TPU v7x, 512 devices: a whole 4x8x8 slice. The times are simulated.
512 devices in a mesh: seq: 64 (over z, y), mp: 4 (over x), dp: 2 (over core).
Axes of the slice: x: 4, y: 8, z: 8, core: 2. Of those that a mesh axis runs over, the one named last changes fastest.
Arguments:
- enc_tokens: bfloat16 [4, 2048, 1280], P('dp', 'seq'), may hold values from -6 to 6
- enc_gain: float32 [1280], replicated, may hold values from 0.4 to 1.6
- enc_bias: float32 [1280], replicated, may hold values from -3 to 3
- w_in: bfloat16 [1280, 2560], P(None, 'mp'), may hold values from -0.15625 to 0.15625
- w_out: bfloat16 [2560, 1280], P('mp'), may hold values from -0.125 to 0.125
- final_gain: float32 [1280], replicated, may hold values from 0.4 to 1.6
- w_embed: bfloat16 [1280, 512], P(None, 'mp'), may hold values from -0.15625 to 0.15625
- dest: int32 [4, 2048, 1], P('dp', 'seq'), may hold values from 0 to 63; in each aligned block of 32 rows (0 to 31, 32 to 63, ..., all dimensions but the last counted through in order) at most 2 rows name the same one
- mask_token: bfloat16 [512], replicated, may hold values from -4 to 4
- dec_gain: float32 [512], replicated, may hold values from 0.4 to 1.6
- w_query: bfloat16 [512, 256], P(None, 'mp'), may hold values from -10 to 10
- w_key: bfloat16 [512, 256], P(None, 'mp'), may hold values from -0.25 to 0.25
- w_value: bfloat16 [512, 256], P(None, 'mp'), may hold values from -0.25 to 0.25
- w_proj: bfloat16 [256, 512], P('mp'), may hold values from -1 to 1
Outputs:
- decoded: bfloat16 [4, 8192, 512], P('dp', ('seq', 'mp'))
Inputs may be any that keep to these rules, and one draw needn't show every extreme that they name: `dest`: in each aligned block of 32 rows of an image (the rows of one index of seq) no tile is named more than 2 times.
All inputs are finite; a program needn't handle non-finite values.
Results may differ from a plain program's by a relative error of at most 0.033.
Values may be sent and summed in bfloat16 or wider, within the bound.
A program may use at most 64 MiB of HBM per device.

v0:
```python
import math

import jax
import jax.numpy as jnp
from jax import lax
from jax.sharding import PartitionSpec as P

HD = 32
PATCH_DEV = 128


def normalize(values):
    average = jnp.mean(values, axis=-1, keepdims=True)
    centered = values - average
    spread = jnp.mean(centered * centered, axis=-1, keepdims=True)
    return centered * lax.rsqrt(spread + 1e-06)


def positions(first, count, width):
    index_values = (first + jnp.arange(count, dtype=jnp.int32)).astype(jnp.float32)
    freqs = 1.0 / 10000.0 ** (jnp.arange(width // 2, dtype=jnp.float32) / (width // 2))
    angle = index_values[:, None] * freqs[None, :]
    return jnp.concatenate([jnp.sin(angle), jnp.cos(angle)], axis=-1)


def local(
    enc_tokens,
    enc_gain,
    enc_bias,
    w_in,
    w_out,
    final_gain,
    w_embed,
    dest,
    mask_token,
    dec_gain,
    w_query,
    w_key,
    w_value,
    w_proj,
):
    images, visible, model_width = enc_tokens.shape
    seq_count = lax.axis_size("seq")
    mp_count = lax.axis_size("mp")
    capacity = PATCH_DEV // seq_count
    dec_width = mask_token.shape[0]
    token_values = enc_tokens.astype(jnp.float32)
    normed = (normalize(token_values) * enc_gain + enc_bias).astype(jnp.bfloat16)
    pre_act = jnp.einsum("ivd,df->ivf", normed, w_in, preferred_element_type=jnp.float32)
    hidden = jax.nn.gelu(pre_act, approximate=False).astype(jnp.bfloat16)
    partial_out = jnp.einsum("ivf,fd->ivd", hidden, w_out, preferred_element_type=jnp.float32)
    mixed = token_values + lax.psum(partial_out, "mp")
    encoded = (normalize(mixed) * final_gain).astype(jnp.bfloat16)
    embedded = jnp.einsum(
        "ivd,de->ive", encoded, w_embed, preferred_element_type=jnp.float32
    ).astype(jnp.bfloat16)
    targets = dest[:, :, 0]
    matching = targets[:, :, None] == targets[:, None, :]
    ordering = jnp.arange(visible, dtype=jnp.int32)
    before = ordering[None, :] < ordering[:, None]
    ranking = jnp.sum(jnp.where(matching & before[None], 1, 0), axis=-1).astype(jnp.int32)
    slot_index = targets * capacity + ranking
    one_hot = (
        slot_index[:, :, None] == jnp.arange(PATCH_DEV, dtype=jnp.int32)[None, None, :]
    ).astype(jnp.bfloat16)
    send_rows = jnp.einsum(
        "ivs,ive->ise", one_hot, embedded, preferred_element_type=jnp.float32
    ).astype(jnp.bfloat16)
    send_flags = jnp.sum(one_hot.astype(jnp.float32), axis=1).astype(jnp.bfloat16)
    row_width = send_rows.shape[2]
    send_rows = send_rows.reshape(images, seq_count, capacity, row_width)
    send_flags = send_flags.reshape(images, seq_count, capacity)
    got_rows, got_flags = (
        lax.all_to_all(send_rows, "seq", split_axis=1, concat_axis=1, tiled=True),
        lax.all_to_all(send_flags, "seq", split_axis=1, concat_axis=1, tiled=True),
    )
    tile_rows = got_rows.reshape(images, PATCH_DEV, row_width)
    present = got_flags.reshape(images, PATCH_DEV)
    full_tile = lax.all_gather(tile_rows, "mp", axis=2, tiled=True)
    first_patch = lax.axis_index("seq") * PATCH_DEV
    dec_x = jnp.where(
        present[:, :, None] > 0,
        full_tile.astype(jnp.float32),
        mask_token.astype(jnp.float32)[None, None, :],
    )
    dec_x = dec_x + positions(first_patch, PATCH_DEV, dec_width)[None]
    dec_norm = (normalize(dec_x) * dec_gain).astype(jnp.bfloat16)
    query = jnp.einsum("ipd,dc->ipc", dec_norm, w_query, preferred_element_type=jnp.float32).astype(
        jnp.bfloat16
    )
    key_rows = jnp.einsum(
        "ipd,dc->ipc", dec_norm, w_key, preferred_element_type=jnp.float32
    ).astype(jnp.bfloat16)
    value_rows = jnp.einsum(
        "ipd,dc->ipc", dec_norm, w_value, preferred_element_type=jnp.float32
    ).astype(jnp.bfloat16)
    heads_here = query.shape[2] // HD
    pairs = jnp.concatenate([key_rows, value_rows], axis=2)
    query_heads = query.reshape(images, PATCH_DEV, heads_here, HD)
    start_state = (
        jnp.full((images, heads_here, PATCH_DEV), -1e30, jnp.float32),
        jnp.zeros((images, heads_here, PATCH_DEV), jnp.float32),
        jnp.zeros((images, heads_here, PATCH_DEV, HD), jnp.float32),
    )
    piece = lax.all_gather(pairs, "seq", axis=1, tiled=True)
    key_count = piece.shape[1]
    block = math.gcd(key_count, 512)
    blocks = piece.reshape(images, key_count // block, block, 2, heads_here, HD)

    def one_step(state, kv_block):
        top_score, total, accum = state
        scores = jnp.einsum(
            "iphd,ibhd->ihpb", query_heads, kv_block[:, :, 0], preferred_element_type=jnp.float32
        ) / math.sqrt(HD)
        new_top = jnp.maximum(top_score, jnp.max(scores, axis=-1))
        correction = jnp.exp(top_score - new_top)
        expo = jnp.exp(scores - new_top[..., None])
        total = total * correction + jnp.sum(expo, axis=-1)
        accum = accum * correction[..., None] + jnp.einsum(
            "ihpb,ibhd->ihpd",
            expo.astype(jnp.bfloat16),
            kv_block[:, :, 1],
            preferred_element_type=jnp.float32,
        )
        return ((new_top, total, accum), None)

    result, unused = lax.scan(one_step, start_state, jnp.moveaxis(blocks, 1, 0))
    top_score, total, accum = result
    attended = (accum / total[..., None]).astype(jnp.bfloat16)
    attended = jnp.transpose(attended, (2, 0, 1, 3)).reshape(PATCH_DEV, images, heads_here * HD)
    row_count = PATCH_DEV // mp_count
    summed = lax.psum_scatter(
        jnp.einsum("pic,cd->pid", attended, w_proj, preferred_element_type=jnp.float32),
        "mp",
        scatter_dimension=0,
        tiled=True,
    )
    residual_rows = lax.dynamic_slice_in_dim(dec_x, lax.axis_index("mp") * row_count, row_count, 1)
    return (residual_rows + jnp.transpose(summed, (1, 0, 2))).astype(jnp.bfloat16)


def solution(mesh):
    placed = (
        P("dp", "seq", None),
        P(),
        P(),
        P(None, "mp"),
        P("mp", None),
        P(),
        P(None, "mp"),
        P("dp", "seq", None),
        P(),
        P(),
        P(None, "mp"),
        P(None, "mp"),
        P(None, "mp"),
        P("mp", None),
    )
    return jax.shard_map(
        local, mesh=mesh, in_specs=placed, out_specs=P("dp", ("seq", "mp"), None), check_vma=False
    )
```

profile of v0, /device:TPU:16, one launch (start us, length us, event | category | flops | bytes accessed | tf_op | source)
XLA Modules:
  0.0 280.3 jit_solution(14587308303673095930)
XLA Ops:
  6.5 1.0 select_reduce_fusion
  7.5 0.7 fusion.85
  8.5 0.7 copy.37
  9.1 16.5 %all-to-all-start = ((bf16[2,64,2]{2,0,1:T(2,128)(2,1)}), bf16[2,64,2]{2,0,1:T(2,128)(2,1)S(1)}, u32[]{:S(2)}, u32[]{:S(2)}) async-start(bf16[2,64,2]{2,0,1:T(2,128)(2,1)} %copy.37), calls=%async_computation | async-start | bytes 65536 | tf_op jit(solution)/shard_map/all_to_all | solution.py:75
  25.7 1.1 convert_reduce_fusion
  26.8 1.1 fusion.13
  27.9 1.4 fusion.79
  29.4 1.4 fusion.7
  30.9 0.5 multiply_sine_fusion
  31.5 4.2 %all-to-all-done = bf16[2,64,2]{2,0,1:T(2,128)(2,1)S(1)} async-done(((bf16[2,64,2]{2,0,1:T(2,128)(2,1)}), bf16[2,64,2]{2,0,1:T(2,128)(2,1)S(1)}, u32[]{:S(2)}, u32[]{:S(2)}) %all-to-all-start) | async-done | bytes 544 | tf_op jit(solution)/shard_map/all_to_all | solution.py:75
  35.8 48.6 %all-reduce.2.cloned.1.call-done = f32[2,32,1280]{2,1,0:T(8,128)} async-done(((f32[2,32,1280]{2,1,0:T(8,128)}), f32[2,32,1280]{2,1,0:T(8,128)}) %all-reduce.2.cloned.1.call-update) | async-done | bytes 327696 | tf_op jit(solution)/shard_map/psum | solution.py:52
  84.4 1.1 fusion.40
  85.5 1.2 multiply_reduce_fusion.1
  86.7 1.4 convolution_convert_fusion
  88.1 0.7 copy.40
  88.7 13.3 %all-to-all-start.1 = ((bf16[2,64,2,128]{3,2,0,1:T(2,128)(2,1)}), bf16[2,64,2,128]{3,2,0,1:T(2,128)(2,1)S(1)}, u32[]{:S(2)}, u32[]{:S(2)}) async-start(bf16[2,64,2,128]{3,2,0,1:T(2,128)(2,1)} %copy.40), calls=%async_computation.1 | async-start | bytes 131072 | tf_op jit(solution)/shard_map/all_to_all | solution.py:74
  102.5 10.2 %all-to-all-done.1 = bf16[2,64,2,128]{3,2,0,1:T(2,128)(2,1)S(1)} async-done(((bf16[2,64,2,128]{3,2,0,1:T(2,128)(2,1)}), bf16[2,64,2,128]{3,2,0,1:T(2,128)(2,1)S(1)}, u32[]{:S(2)}, u32[]{:S(2)}) %all-to-all-start.1) | async-done | bytes 65568 | tf_op jit(solution)/shard_map/all_to_all | solution.py:74
  112.7 11.7 %all_gather.6 = bf16[2,128,512]{2,1,0:T(8,128)(2,1)S(1)} all-gather(bf16[2,128,128]{2,1,0:T(8,128)(2,1)S(1)} %bitcast.80), channel_id=1, replica_groups=mesh['seq'=64,'mp'=4,'dp'=2] {'mp'}, dimensions={2}, use_global_device_ids=true | all-gather | bytes 327680 | tf_op jit(solution)/shard_map/all_gather | solution.py:79
  125.4 0.6 pad_maximum_fusion.1
  126.4 83.2 %all-gather.2.cloned.1.call-done = bf16[2,8192,128]{1,2,0:T(8,128)(2,1)} async-done(((bf16[2,128,128]{1,2,0:T(8,128)(2,1)}), bf16[2,8192,128]{1,2,0:T(8,128)(2,1)}) %all-gather.2.cloned.1.call-update) | async-done | bytes 4194320 | tf_op jit(solution)/shard_map/all_gather | solution.py:105
  209.6 4.0 %copy.44 = bf16[32,8,16,512]{3,2,1,0:T(8,128)(2,1)S(1)} copy(bf16[32,8,16,512]{3,1,2,0:T(8,128)(2,1)} %bitcast.78) | data formatting | bytes 8388608
  213.6 4.3 %copy.46 = bf16[2,16,512,2,2,32]{2,5,4,0,3,1:T(8,128)(2,1)} copy(bf16[2,16,512,2,2,32]{2,1,5,4,3,0:T(8,128)(2,1)S(1)} %bitcast.76) | data formatting | bytes 8388608 | tf_op jit(solution)/shard_map/reshape | solution.py:108
  218.0 29.8 %while.15 = (s32[]{:T(128)}, f32[2,2,128]{2,1,0:T(2,128)S(1)}, f32[2,2,128]{2,1,0:T(2,128)S(1)}, f32[2,2,128,32]{2,3,1,0:T(8,128)S(1)}, bf16[16,2,512,2,2,32]{2,...) while((s32[]{:T(128)}, f32[2,2,128]{2,1,0:T(2,128)S(1)}, ...), condition=%wide.region_12.13_spmd.clone, body=%wide.region_9.12_spmd.clone.sunk | while | flops 35179008 | bytes 4128877 | solution.py:127
  218.0 1.0 dynamic-slice_bitcast_fusion.2
  219.0 0.4 fusion.132
  219.9 1.0 dynamic-slice_bitcast_fusion.2
  220.8 0.4 fusion.132
  221.7 1.0 dynamic-slice_bitcast_fusion.2
  222.7 0.4 fusion.132
  223.6 1.0 dynamic-slice_bitcast_fusion.2
  224.6 0.4 fusion.132
  225.5 1.0 dynamic-slice_bitcast_fusion.2
  226.4 0.4 fusion.132
  227.3 1.0 dynamic-slice_bitcast_fusion.2
  228.3 0.4 fusion.132
  228.9 0.3 convolution_add_fusion.2
  229.2 1.0 dynamic-slice_bitcast_fusion.2
  230.2 0.4 fusion.132
  230.7 0.3 convolution_add_fusion.2
  231.1 1.0 dynamic-slice_bitcast_fusion.2
  232.0 0.4 fusion.132
  232.9 1.0 dynamic-slice_bitcast_fusion.2
  233.9 0.4 fusion.132
  234.5 0.3 convolution_add_fusion.2
  234.8 1.0 dynamic-slice_bitcast_fusion.2
  235.8 0.4 fusion.132
  236.6 1.0 dynamic-slice_bitcast_fusion.2
  237.6 0.4 fusion.132
  238.5 1.0 dynamic-slice_bitcast_fusion.2
  239.5 0.4 fusion.132
  240.0 0.3 convolution_add_fusion.2
  240.4 1.0 dynamic-slice_bitcast_fusion.2
  241.3 0.4 fusion.132
  241.9 0.3 convolution_add_fusion.2
  242.2 1.0 dynamic-slice_bitcast_fusion.2
  243.2 0.4 fusion.132
  243.8 0.3 convolution_add_fusion.2
  244.1 1.0 dynamic-slice_bitcast_fusion.2
  245.1 0.4 fusion.132
  246.0 1.0 dynamic-slice_bitcast_fusion.2
  246.9 0.4 fusion.132
  247.9 1.0 fusion.73
  248.9 23.3 %reduce-scatter.2.cloned.1.call-done = f32[32,2,512]{2,0,1:T(8,128)} async-done(((f32[128,2,512]{2,0,1:T(8,128)}), f32[32,2,512]{2,0,1:T(8,128)}) %reduce-scatter.2.cloned.1.call-update) | async-done | bytes 131088 | tf_op jit(solution)/shard_map/reduce_scatter | solution.py:132
  272.2 1.6 fusion.39
  (130 shorter events, 8.2 us)
Async XLA Ops:
  6.5 21.4 %copy-start = (bf16[1280,640]{1,0:T(8,128)(2,1)S(1)}, bf16[1280,640]{1,0:T(8,128)(2,1)}, u32[]{:S(2)}) copy-start(bf16[1280,640]{1,0:T(8,128)(2,1)} %param.19) | copy-start | bytes 4915204
  9.1 26.6 %all-to-all-start = ((bf16[2,64,2]{2,0,1:T(2,128)(2,1)}), bf16[2,64,2]{2,0,1:T(2,128)(2,1)S(1)}, u32[]{:S(2)}, u32[]{:S(2)}) async-start(bf16[2,64,2]{2,0,1:T(2,128)(2,1)} %copy.37), calls=%async_computation | async-start | bytes 65536 | tf_op jit(solution)/shard_map/all_to_all | solution.py:75
  25.6 58.8 %all-reduce.2.cloned.1.call-start = ((), (), s32[]{:S(2)}) async-start(), calls=%async_computation.3 | async-start | bytes 655360 | tf_op jit(solution)/shard_map/psum | solution.py:52
  25.7 3.7 %copy-start.10 = (bf16[640,1280]{1,0:T(8,128)(2,1)S(1)}, bf16[640,1280]{1,0:T(8,128)(2,1)}, u32[]{:S(2)}) copy-start(bf16[640,1280]{1,0:T(8,128)(2,1)} %param.20) | copy-start | bytes 4915204
  29.4 2.1 copy-start.9
  29.4 55.0 %copy-start.1 = (bf16[2,32,1280]{2,1,0:T(8,128)(2,1)S(1)}, bf16[2,32,1280]{2,1,0:T(8,128)(2,1)}, u32[]{:S(2)}) copy-start(bf16[2,32,1280]{2,1,0:T(8,128)(2,1)} %param.16) | copy-start | bytes 491524
  30.8 55.9 %copy-start.2 = (bf16[1280,128]{1,0:T(8,128)(2,1)S(1)}, bf16[1280,128]{1,0:T(8,128)(2,1)}, u32[]{:S(2)}) copy-start(bf16[1280,128]{1,0:T(8,128)(2,1)} %param.22) | copy-start | bytes 983044
  30.8 55.9 %copy-start.7 = (f32[1280]{0:T(1024)S(1)}, f32[1280]{0:T(1024)}, u32[]{:S(2)}) copy-start(f32[1280]{0:T(1024)} %param.21) | copy-start | bytes 15364
  86.7 38.2 %copy-start.8 = (f32[512]{0:T(512)S(1)}, f32[512]{0:T(512)}, u32[]{:S(2)}) copy-start(f32[512]{0:T(512)} %param.25) | copy-start | bytes 6148
  88.1 36.9 %copy-start.4 = (bf16[512,64]{0,1:T(8,128)(2,1)S(1)}, bf16[512,64]{0,1:T(8,128)(2,1)}, u32[]{:S(2)}) copy-start(bf16[512,64]{0,1:T(8,128)(2,1)} %param.28) | copy-start | bytes 196612
  88.7 23.9 %all-to-all-start.1 = ((bf16[2,64,2,128]{3,2,0,1:T(2,128)(2,1)}), bf16[2,64,2,128]{3,2,0,1:T(2,128)(2,1)S(1)}, u32[]{:S(2)}, u32[]{:S(2)}) async-start(bf16[2,64,2,128]{3,2,0,1:T(2,128)(2,1)} %copy.40), calls=%async_computation.1 | async-start | bytes 131072 | tf_op jit(solution)/shard_map/all_to_all | solution.py:74
  102.1 23.1 %copy-start.5 = (bf16[512,64]{0,1:T(8,128)(2,1)S(1)}, bf16[512,64]{0,1:T(8,128)(2,1)}, u32[]{:S(2)}) copy-start(bf16[512,64]{0,1:T(8,128)(2,1)} %param.27) | copy-start | bytes 196612
  102.1 107.5 %all-gather.2.cloned.1.call-start = ((), (), s32[]{:S(2)}) async-start(), calls=%async_computation.4 | async-start | bytes 4259840 | tf_op jit(solution)/shard_map/all_gather | solution.py:105
  124.4 1.8 copy-start.6
  126.1 146.1 %reduce-scatter.2.cloned.1.call-start = ((), (), s32[]{:S(2)}) async-start(), calls=%async_computation.5 | async-start | bytes 655360 | tf_op jit(solution)/shard_map/reduce_scatter | solution.py:132
  218.0 29.9 %copy-start.3 = (bf16[64,512]{1,0:T(8,128)(2,1)S(1)}, bf16[64,512]{1,0:T(8,128)(2,1)}, u32[]{:S(2)}) copy-start(bf16[64,512]{1,0:T(8,128)(2,1)} %param.29) | copy-start | bytes 196612
Sparse Core Ops, SparseCore 0:
  31.0 53.3 all-reduce.1
  126.2 83.3 all-gather.1
  249.0 23.1 reduce-scatter.1
where the time goes:
time: 281 us; the launch traced here: 280 us
  waiting for transfers between devices  170 us (60%)
  starting transfers between devices  29.9 us (11%)
  local copies, waits for them, and re-layouts  25.9 us (9%)
  matrix products  16.5 us (6%)
  between operations  13.4 us (5%)
  other arithmetic  12.7 us (5%)
  blocking collectives  11.7 us (4%)
    all_gather x1, waiting for transfers between devices, local(): piece = lax.all_gather(pairs, 'seq', axis=1, tiled=True)  83.2 us
    psum x1, waiting for transfers between devices, local(): mixed = token_values + lax.psum(partial_out, 'mp')  48.6 us
    reduce_scatter x1, waiting for transfers between devices, local(): lax.psum_scatter(jnp.einsum('pic,cd->pid', attended, w_proj, preferred_el...  23.3 us
    all_to_all x1, starting transfers between devices, local(): lax.all_to_all(send_flags, 'seq', split_axis=1, concat_axis=1, tiled=True)  16.5 us
    squeeze x16, local copies, waits for them, and re-layouts, local(): result, unused = lax.scan(one_step, start_state, jnp.moveaxis(blocks, 1, 0))  15.6 us
    all_to_all x1, starting transfers between devices, local(): lax.all_to_all(send_rows, 'seq', split_axis=1, concat_axis=1, tiled=True)  13.3 us
    all_gather x1, blocking collectives, local(): full_tile = lax.all_gather(tile_rows, 'mp', axis=2, tiled=True)  11.7 us
    all_to_all x1, waiting for transfers between devices, local(): lax.all_to_all(send_rows, 'seq', split_axis=1, concat_axis=1, tiled=True)  10.2 us
  transfers between devices with their start and end apart: 5, of which 5 were waited for; matrix products, arithmetic and copies ran while one was open for 2% of the time, Pallas kernels for 0%

commit v1 on v0

v1 whole, which is shorter than its diff:
```python
import functools
import math

import jax
import jax.numpy as jnp
import numpy as np
from jax import lax
from jax.experimental import pallas as pl
from jax.experimental.pallas import tpu as pltpu
from jax.sharding import PartitionSpec as P

HD = 32
TILE = 128
BIG = -1e30
MESH = pl.DeviceIdType.MESH
F32 = jnp.float32
BF16 = jnp.bfloat16


def contract_last(left, right):
    return lax.dot_general(left, right, (((1,), (1,)), ((), ())), preferred_element_type=F32)


def matmul(left, right):
    return jnp.dot(left, right, preferred_element_type=F32)


def normalize(values):
    average = jnp.mean(values, axis=-1, keepdims=True)
    centered = values - average
    spread = jnp.mean(centered * centered, axis=-1, keepdims=True)
    return centered * lax.rsqrt(spread + 1e-06)


def iota(shape, dim):
    return lax.broadcasted_iota(jnp.int32, shape, dim)


def waves(count, scale, width):
    half = width // 2
    freqs = 1.0 / 10000.0 ** (np.arange(half, dtype=np.float64) / half)
    angle = (np.arange(count, dtype=np.float64) * scale)[:, None] * freqs[None, :]
    return np.concatenate([np.sin(angle), np.cos(angle)], axis=-1).astype(np.float32)


def turned(first, second):
    half = first.shape[-1] // 2
    sin_a, cos_a = first[:, :half], first[:, half:]
    sin_b, cos_b = second[:, :half], second[:, half:]
    return jnp.concatenate([sin_a * cos_b + cos_a * sin_b, cos_a * cos_b - sin_a * sin_b], axis=-1)


def picked(one_hot, table):
    high = table.astype(BF16)
    low = (table - high.astype(F32)).astype(BF16)
    return matmul(one_hot, high) + matmul(one_hot, low)


def kernel(
    cfg,
    tok_ref,
    gain_ref,
    bias_ref,
    w_in_hbm,
    w_out_hbm,
    final_ref,
    w_embed_hbm,
    dest_ref,
    mask_ref,
    dec_gain_ref,
    wq_ref,
    wk_ref,
    wv_ref,
    w_proj_ref,
    waves_hbm,
    near_ref,
    far_ref,
    rot_ref,
    perm_ref,
    out_ref,
    w_in,
    w_out,
    w_embed,
    wave_t,
    part_own,
    part_send,
    rs_recv,
    enc_all,
    e_all,
    a_src,
    a_y,
    a_mid,
    a_z,
    q_src,
    q_y,
    q_mid,
    q_z,
    kv,
    kt,
    kb,
    vt,
    res_recv,
    tile_pos,
    stat_w,
    pr_own,
    pr_send,
    pr_recv,
    local_sem,
    x_send,
    x_recv,
    y_send,
    y_recv,
    z_send,
    z_recv,
):
    nx, ny, nz, images, vis = cfg
    tiles = ny * nz
    cap = TILE // tiles
    rows = images * vis
    block_rows = rows // nx
    width = out_ref.shape[2]
    cols = wq_ref.shape[1]
    own_rows = TILE // nx
    seq = lax.axis_index("seq")
    mx = lax.axis_index("mp")
    z, y = seq // ny, seq % ny

    loads = []
    for number, (src, dst) in enumerate(
        ((w_in_hbm, w_in), (w_out_hbm, w_out), (w_embed_hbm, w_embed), (waves_hbm, wave_t))
    ):
        load = pltpu.make_async_copy(src, dst, local_sem.at[number])
        load.start()
        loads.append(load)

    def partner(axis, d):
        if axis == "x":
            index = lax.rem(mx + d, nx)
            return index, {"mp": index}
        if axis == "y":
            index = lax.rem(y + d, ny)
            return index, {"seq": z * ny + index}
        index = lax.rem(z + d, nz)
        return index, {"seq": index * ny + y}

    sizes = {"x": nx, "y": ny, "z": nz}
    places = {"x": mx, "y": y, "z": z}
    sems = {"x": (x_send, x_recv), "y": (y_send, y_recv), "z": (z_send, z_recv)}
    barrier = pltpu.get_barrier_semaphore()
    for axis in "xyz":
        for d in range(1, sizes[axis]):
            pl.semaphore_signal(barrier, inc=1, device_id=partner(axis, d)[1], device_id_type=MESH)

    pending = []

    def order(size):
        return sorted(range(1, size), key=lambda d: -min(d, size - d))

    def exchange(axis, group, source, target):
        size = sizes[axis]
        send, recv = sems[axis]
        for d in order(size):
            index, device = partner(axis, d)
            copy = pltpu.make_async_remote_copy(
                src_ref=source(index),
                dst_ref=target(places[axis], d),
                send_sem=send.at[group, d - 1],
                recv_sem=recv.at[group, d - 1],
                device_id=device,
                device_id_type=MESH,
            )
            copy.start()
            pending.append(copy)

        def arrived(d):
            sender, device = partner(axis, size - d)
            pltpu.make_async_remote_copy(
                src_ref=target(sender, d),
                dst_ref=target(sender, d),
                send_sem=send.at[group, d - 1],
                recv_sem=recv.at[group, d - 1],
                device_id=device,
                device_id_type=MESH,
            ).wait_recv()

        def all_arrived():
            for d in range(1, size):
                arrived(d)

        return all_arrived

    def part_of(ref, count):
        return lambda index, d=0: ref.at[pl.ds(pl.multiple_of(index * count, count), count)]

    tokens = tok_ref[...].astype(F32)
    normed = (normalize(tokens) * gain_ref[...][None, :] + bias_ref[...][None, :]).astype(BF16)
    loads[0].wait()
    pre = matmul(normed, w_in[...])
    hidden = (0.5 * pre * (1.0 + lax.erf(pre * math.sqrt(0.5)))).astype(BF16)
    loads[1].wait()
    partial = matmul(hidden, w_out[...])
    part_own[...] = partial
    part_send[...] = partial.astype(BF16)
    pl.semaphore_wait(barrier, (nx - 1) + (ny - 1) + (nz - 1))
    rs_done = exchange("x", 0, part_of(part_send, block_rows), lambda index, d: rs_recv.at[d - 1])

    dest_col = dest_ref[...]
    eye = iota((rows, rows), 0) == iota((rows, rows), 1)
    dest_row = jnp.sum(jnp.where(eye, dest_col, 0), axis=0, keepdims=True)
    same = (dest_col == dest_row) & (iota((rows, rows), 0) // vis == iota((rows, rows), 1) // vis)
    rank_col = jnp.sum(
        jnp.where(same & (iota((rows, rows), 1) < iota((rows, rows), 0)), 1, 0), axis=1, keepdims=True
    )
    rank_row = jnp.sum(
        jnp.where(same & (iota((rows, rows), 0) < iota((rows, rows), 1)), 1, 0), axis=0, keepdims=True
    )
    slot_col = dest_col * cap + rank_col
    hits = jnp.where(slot_col == iota((rows, TILE), 1), 1.0, 0.0)
    flag_rows = jnp.zeros((16, TILE), F32)
    for i in range(images):
        count = jnp.sum(hits[i * vis : (i + 1) * vis], axis=0, keepdims=True)
        flag_rows = jnp.where(iota((16, TILE), 0) == i, count, flag_rows)

    def flag_lanes(count):
        return lambda index, d=0: kb.at[:, pl.ds(pl.multiple_of(index * count, TILE), count)]

    kb[:, pl.ds(pl.multiple_of(seq * TILE, TILE), TILE)] = (flag_rows * BIG).astype(BF16)
    flags_y = exchange(
        "y", 0, lambda index: flag_lanes(TILE)(seq), lambda index, d: flag_lanes(TILE)(z * ny + index)
    )
    order_row = ((dest_row % ny) * nz + dest_row // ny) * cap + rank_row
    spread_f = jnp.where(order_row == iota((TILE, rows), 0), 1.0, 0.0)
    lane_image = iota((TILE, rows), 1) // vis
    spreads = [jnp.where(lane_image == i, spread_f, 0.0) for i in range(images)]
    taken = [jnp.sum(one, axis=1, keepdims=True) for one in spreads]
    spreads = [one.astype(BF16) for one in spreads]

    at_tile = jnp.where(dest_col == iota((rows, tiles), 1), 1.0, 0.0).astype(BF16)
    at_place = jnp.where(seq * cap + rank_col == iota((rows, TILE), 1), 1.0, 0.0).astype(BF16)
    vis_pos = turned(picked(at_tile, far_ref[...]), picked(at_place, near_ref[...]))
    tile_pos[...] = turned(near_ref[...], far_ref[pl.ds(seq, 1), :])

    mask = mask_ref[...].astype(F32)[None, :]
    dec_gain = dec_gain_ref[...][None, :]
    mask_mid = mask - jnp.mean(mask, axis=-1, keepdims=True)
    mask_spread = jnp.mean(mask_mid * mask_mid, axis=-1, keepdims=True) + 0.5
    weights = jnp.concatenate([wk_ref[...], wv_ref[...]], axis=1)
    kv_cols = 2 * cols
    eye_w = jnp.where(iota((kv_cols, kv_cols), 0) == iota((kv_cols, kv_cols), 1), 1.0, 0.0).astype(BF16)
    gained = contract_last(eye_w, weights) * dec_gain
    stat_w[0:kv_cols, :] = gained
    gain_sum = jnp.sum(gained, axis=1, keepdims=True)
    mask_sum = jnp.sum(gained * mask_mid, axis=1, keepdims=True)
    stat_rows = iota((16, width), 0)
    stat_w[kv_cols:, :] = jnp.where(stat_rows == 0, 1.0, jnp.where(stat_rows == 1, mask_mid, 0.0)) * (1.0 / width)
    lanes = wave_t.shape[1]
    loads[3].wait()
    half = width // 2

    def table_step(step, carry):
        turn = rot_ref[pl.ds(step, 1), :]
        sin_t, cos_t = turn[:, :half], turn[:, half:]
        sin_w, cos_w = stat_w[:, :half], stat_w[:, half:]
        rotated = jnp.concatenate(
            [(sin_w * cos_t - cos_w * sin_t).astype(BF16), (sin_w * sin_t + cos_w * cos_t).astype(BF16)], axis=1
        )
        found = matmul(rotated, wave_t[...])
        average = found[kv_cols : kv_cols + 1]
        spread = mask_spread + 2.0 * found[kv_cols + 1 : kv_cols + 2] - average * average
        scale = lax.rsqrt(jnp.maximum(spread, 0.0) + 1e-06)
        made = ((found[:kv_cols] + mask_sum - average * gain_sum) * scale).astype(BF16)
        where = pl.ds(pl.multiple_of(step * lanes, lanes), lanes)
        kt[:, where] = made[:cols]
        vt[:, where] = made[cols:]
        return carry

    steps = rot_ref.shape[0]
    cut = [0, steps * 3 // 8, steps * 6 // 8, steps]
    lax.fori_loop(cut[0], cut[1], table_step, 0)

    rs_done()
    mine = pl.ds(pl.multiple_of(mx * block_rows, block_rows), block_rows)
    mixed = tok_ref[mine, :].astype(F32) + part_own[mine, :]
    for d in range(nx - 1):
        mixed = mixed + rs_recv[d].astype(F32)
    enc_all[mine, :] = (normalize(mixed) * final_ref[...][None, :]).astype(BF16)
    enc_done = exchange(
        "x", 1, lambda index: part_of(enc_all, block_rows)(mx), lambda index, d: part_of(enc_all, block_rows)(index)
    )
    lax.fori_loop(cut[1], cut[2], table_step, 0)
    flags_y()
    flags_z = exchange(
        "z", 0, lambda index: flag_lanes(TILE * ny)(z), lambda index, d: flag_lanes(TILE * ny)(index)
    )
    loads[2].wait()
    enc_done()
    embedded = matmul(enc_all[...], w_embed[...]).astype(BF16)
    e_all[mx] = embedded
    e_done = exchange("x", 2, lambda index: e_all.at[mx], lambda index, d: e_all.at[index])
    ry, rz = nz * cap, ny * cap
    a_src[...] = jnp.concatenate([matmul(one, embedded) for one in spreads], axis=1).astype(BF16)

    def first_leg(group, src, mid):
        done = exchange("y", group, part_of(src, ry), part_of(mid, ry))
        mid[pl.ds(pl.multiple_of(y * ry, ry), ry), :] = src[pl.ds(pl.multiple_of(y * ry, ry), ry), :]
        return done

    def second_leg(group, mid, turned_ref, final):
        turned_ref[...] = matmul(perm_ref[...], mid[...]).astype(BF16)
        done = exchange("z", group, part_of(turned_ref, rz), part_of(final, rz))
        final[pl.ds(pl.multiple_of(z * rz, rz), rz), :] = turned_ref[pl.ds(pl.multiple_of(z * rz, rz), rz), :]
        return done

    a_first = first_leg(1, a_src, a_y)
    lax.fori_loop(cut[2], cut[3], table_step, 0)

    score_scale = math.log2(math.e) / math.sqrt(HD)
    mask_rows = (normalize(mask + tile_pos[...]) * dec_gain).astype(BF16)
    mask_query = matmul(mask_rows, wq_ref[...]) * score_scale

    e_done()
    full = jnp.concatenate([e_all[i] for i in range(nx)], axis=1).astype(F32)
    vis_rows = (normalize(full + vis_pos) * dec_gain).astype(BF16)
    vis_kv = jnp.concatenate([matmul(vis_rows, wv_ref[...]), matmul(vis_rows, wk_ref[...])], axis=1).astype(BF16)
    kv[0, pl.ds(pl.multiple_of(seq * vis, vis), vis), :] = vis_kv[:vis]
    kv[1, pl.ds(pl.multiple_of((y * nz + z) * vis, vis), vis), :] = vis_kv[vis:]
    query = (matmul(vis_rows, wq_ref[...]) * score_scale).astype(BF16)
    q_src[...] = jnp.concatenate(
        [matmul(one, query) for one in spreads]
        + [jnp.broadcast_to(one, (TILE, cols)) for one in taken],
        axis=1,
    ).astype(BF16)
    q_first = first_leg(2, q_src, q_y)
    kv0, kv1 = part_of(kv.at[0], vis), part_of(kv.at[1], vis)
    kv0_first = exchange("y", 3, lambda index: kv0(seq), lambda index, d: kv0(z * ny + index))
    kv1_first = exchange("z", 3, lambda index: kv1(y * nz + z), lambda index, d: kv1(y * nz + index))
    a_first()
    a_second = second_leg(1, a_y, a_mid, a_z)
    q_first()
    q_second = second_leg(2, q_y, q_mid, q_z)
    kv0_first()
    kv0_many = part_of(kv.at[0], vis * ny)
    kv0_second = exchange("z", 4, lambda index: kv0_many(z), lambda index, d: kv0_many(index))
    kv1_first()
    kv1_many = part_of(kv.at[1], vis * nz)
    kv1_second = exchange("y", 4, lambda index: kv1_many(y), lambda index, d: kv1_many(index))

    a_second()
    res_done = exchange("x", 3, part_of(a_z, own_rows), lambda index, d: res_recv.at[index])
    res_recv[mx] = a_z[pl.ds(pl.multiple_of(mx * own_rows, own_rows), own_rows), :]

    flags_z()
    q_second()
    lane = iota((TILE, cols), 1)
    head_masks = [jnp.where(lane // HD == h, 1.0, 0.0) for h in range(cols // HD)]
    heads = len(head_masks)
    found_q = q_z[...]
    states = []
    block = 1024 if tiles * TILE % 1024 == 0 else tiles * TILE
    stacked = []
    for i in range(images):
        present = found_q[:, (images + i) * cols : (images + i + 1) * cols].astype(F32)
        here = jnp.where(present > 0, found_q[:, i * cols : (i + 1) * cols].astype(F32), mask_query)
        stacked.append(jnp.concatenate([here * one for one in head_masks], axis=0).astype(BF16))

    def fold(state, scores, values_of):
        top, total, accum = state
        new_top = jnp.maximum(top, jnp.max(scores, axis=1, keepdims=True))
        fix = jnp.exp2(top - new_top)
        expo = jnp.exp2(scores - new_top)
        total = total * fix + jnp.sum(expo, axis=1, keepdims=True)
        accum = accum * fix + values_of(expo.astype(BF16))
        return new_top, total, accum

    for i in range(images):
        select = jnp.where(iota((heads * TILE, 16), 1) == i, 1.0, 0.0).astype(BF16)
        lookup = jnp.concatenate([stacked[i], select], axis=1)

        def masked_block(number, state):
            where = pl.ds(pl.multiple_of(number * block, block), block)
            scores = matmul(lookup, jnp.concatenate([kt[:, where], kb[:, where]], axis=0))
            return fold(state, scores, lambda expo: contract_last(expo, vt[:, where]))

        start = (
            jnp.full((heads * TILE, 1), BIG, F32),
            jnp.zeros((heads * TILE, 1), F32),
            jnp.zeros((heads * TILE, cols), F32),
        )
        states.append(lax.fori_loop(0, tiles * TILE // block, masked_block, start))

    vis_block = min(1024, tiles * vis)
    projected = []
    rs2 = []
    for i in range(images):
        (kv0_second if i == 0 else kv1_second)()
        lookup = jnp.concatenate([jnp.zeros_like(stacked[i]), stacked[i]], axis=1)

        def visible_block(number, state):
            pairs = kv[i, pl.ds(pl.multiple_of(number * vis_block, vis_block), vis_block), :]
            scores = contract_last(lookup, pairs)
            return fold(state, scores, lambda expo: matmul(expo, pairs)[:, :cols])

        top, total, accum = lax.fori_loop(0, tiles * vis // vis_block, visible_block, states[i])
        accum = accum / total
        attended = jnp.zeros((TILE, cols), F32)
        for h in range(heads):
            attended = attended + accum[h * TILE : (h + 1) * TILE] * head_masks[h]
        result = matmul(attended.astype(BF16), w_proj_ref[...])
        pr_own[i] = result
        pr_send[i] = result.astype(BF16)
        rs2.append(
            exchange("x", 4 + i, part_of(pr_send.at[i], own_rows), lambda index, d, i=i: pr_recv.at[d - 1, i])
        )

    res_done()
    tile_mine = pl.ds(pl.multiple_of(mx * own_rows, own_rows), own_rows)
    my_flags = q_z[tile_mine, :].astype(F32)
    my_pos = tile_pos[tile_mine, :]
    chunk = width // nx
    for i in range(images):
        rows_here = jnp.concatenate(
            [res_recv[j, :, i * chunk : (i + 1) * chunk] for j in range(nx)], axis=1
        ).astype(F32)
        start_lane = (images + i) * cols
        present = my_flags[:, start_lane : start_lane + 1]
        value = jnp.where(present > 0, rows_here, mask) + my_pos + pr_own[i, tile_mine, :]
        rs2[i]()
        for d in range(nx - 1):
            value = value + pr_recv[d, i].astype(F32)
        out_ref[i] = value.astype(BF16)
    for copy in pending:
        copy.wait_send()


def local(
    enc_tokens,
    enc_gain,
    enc_bias,
    w_in,
    w_out,
    final_gain,
    w_embed,
    dest,
    mask_token,
    dec_gain,
    w_query,
    w_key,
    w_value,
    w_proj,
):
    images, vis, model_width = enc_tokens.shape
    seq_count = lax.axis_size("seq")
    nx = lax.axis_size("mp")
    ny = math.isqrt(seq_count)
    nz = seq_count // ny
    width = mask_token.shape[0]
    cols = w_query.shape[1]
    cap = TILE // seq_count
    rows = images * vis
    own = TILE // nx
    patches = seq_count * TILE

    low = min(4, seq_count // 2)
    s_low, t, c = np.meshgrid(np.arange(low), np.arange(seq_count), np.arange(cap), indexing="ij")
    place = (s_low * cap + t * TILE + c).reshape(-1)
    wave_t = waves(int(place.max()) + 1, 1, width)[place].T.astype(jnp.bfloat16)
    near = waves(TILE, 1, width)
    far = waves(seq_count, TILE, width)
    rot = waves(seq_count // low, low * cap, width)
    zi, yi, ci = np.meshgrid(np.arange(nz), np.arange(ny), np.arange(cap), indexing="ij")
    perm = np.zeros((TILE, TILE), np.float32)
    perm[np.arange(TILE), ((yi * nz + zi) * cap + ci).reshape(-1)] = 1.0

    hbm = pl.BlockSpec(memory_space=pl.ANY)
    vmem = pl.BlockSpec(memory_space=pltpu.VMEM)
    block_rows = rows // nx
    dma = pltpu.SemaphoreType.DMA
    scratch = [
        pltpu.VMEM(w_in.shape, BF16),
        pltpu.VMEM(w_out.shape, BF16),
        pltpu.VMEM(w_embed.shape, BF16),
        pltpu.VMEM(wave_t.shape, BF16),
        pltpu.VMEM((rows, model_width), F32),
        pltpu.VMEM((rows, model_width), BF16),
        pltpu.VMEM((nx - 1, block_rows, model_width), BF16),
        pltpu.VMEM((rows, model_width), BF16),
        pltpu.VMEM((nx, rows, width // nx), BF16),
        *[pltpu.VMEM((TILE, images * width // nx), BF16)] * 4,
        *[pltpu.VMEM((TILE, 2 * images * cols), BF16)] * 4,
        pltpu.VMEM((images, seq_count * vis, 2 * cols), BF16),
        pltpu.VMEM((cols, patches), BF16),
        pltpu.VMEM((16, patches), BF16),
        pltpu.VMEM((cols, patches), BF16),
        pltpu.VMEM((nx, own, images * width // nx), BF16),
        pltpu.VMEM((TILE, width), F32),
        pltpu.VMEM((2 * cols + 16, width), F32),
        pltpu.VMEM((images, TILE, width), F32),
        pltpu.VMEM((images, TILE, width), BF16),
        pltpu.VMEM((nx - 1, images, own, width), BF16),
        dma((4,)),
        dma((6, nx - 1)),
        dma((6, nx - 1)),
        dma((5, ny - 1)),
        dma((5, ny - 1)),
        dma((5, nz - 1)),
        dma((5, nz - 1)),
    ]
    return pl.pallas_call(
        functools.partial(kernel, (nx, ny, nz, images, vis)),
        out_shape=jax.ShapeDtypeStruct((images, own, width), BF16),
        in_specs=[
            vmem, vmem, vmem, hbm, hbm, vmem, hbm, vmem, vmem, vmem, vmem, vmem, vmem, vmem,
            hbm, vmem, vmem, vmem, vmem,
        ],
        out_specs=vmem,
        scratch_shapes=scratch,
        compiler_params=pltpu.CompilerParams(
            collective_id=0, has_side_effects=True, vmem_limit_bytes=50 * 2**20
        ),
    )(
        enc_tokens.reshape(rows, model_width),
        enc_gain,
        enc_bias,
        w_in,
        w_out,
        final_gain,
        w_embed,
        dest.reshape(rows, 1),
        mask_token,
        dec_gain,
        w_query,
        w_key,
        w_value,
        w_proj,
        jnp.asarray(wave_t),
        jnp.asarray(near),
        jnp.asarray(far),
        jnp.asarray(rot),
        jnp.asarray(perm, BF16),
    )


def solution(mesh):
    placed = (
        P("dp", "seq", None),
        P(),
        P(),
        P(None, "mp"),
        P("mp", None),
        P(),
        P(None, "mp"),
        P("dp", "seq", None),
        P(),
        P(),
        P(None, "mp"),
        P(None, "mp"),
        P(None, "mp"),
        P("mp", None),
    )
    return jax.shard_map(
        local, mesh=mesh, in_specs=placed, out_specs=P("dp", ("seq", "mp"), None), check_vma=False
    )
```

time: 281 us -> 75.2 us (0.27)
  the two profiles are of different devices: /device:TPU:16 before, /device:TPU:8 now
where the time goes in v1:
time: 75.2 us; the launch traced here: 74.4 us
  Pallas kernels  56.9 us (76%)
  local copies, waits for them, and re-layouts  16.1 us (21%)
  other arithmetic  1.34 us (2%)
    pallas_call x1, Pallas kernels, local(): pl.pallas_call(functools.partial(kernel, (nx, ny, nz, images, vis)), out_...  56.9 us
    unnamed x33, local copies, waits for them, and re-layouts  16 us

profile of v1, /device:TPU:8, one launch (start us, length us, event | category | flops | bytes accessed | tf_op | source)
XLA Modules:
  0.0 74.4 jit_solution(18146039968147242744)
XLA Ops:
  0.0 0.5 broadcast.3
  0.5 1.3 %reduce.3 = s32[2,32]{1,0:T(2,128)S(1)} reduce(s32[2,32,1]{1,2,0:T(1,128)} %param.26, s32[]{:T(128)} %broadcast.3), dimensions={2}, to_apply=%param.26.reduce_sub_computation.3 | reduce | bytes 516 | tf_op args[7]
  1.9 0.1 reshape.8.dest_ref
  2.0 1.0 %copy.21.wq_ref = bf16[512,64]{1,0:T(8,128)(2,1)S(1)} copy(bf16[512,64]{0,1:T(8,128)(2,1)} %param.29) | data formatting | bytes 131072 | tf_op args[10]
  2.9 1.0 %copy.22.wk_ref = bf16[512,64]{1,0:T(8,128)(2,1)S(1)} copy(bf16[512,64]{0,1:T(8,128)(2,1)} %param.30) | data formatting | bytes 131072 | tf_op args[11]
  3.9 1.0 %copy.23.wv_ref = bf16[512,64]{1,0:T(8,128)(2,1)S(1)} copy(bf16[512,64]{0,1:T(8,128)(2,1)} %param.31) | data formatting | bytes 131072 | tf_op args[12]
  4.9 0.0 copy-start
  4.9 1.4 %copy-done = bf16[1280,640]{1,0:T(8,128)(2,1)S(1)} copy-done((bf16[1280,640]{1,0:T(8,128)(2,1)S(1)}, bf16[1280,640]{1,0:T(8,128)(2,1)}, u32[]{:S(2)}) %copy-start) | copy-done | bytes 1638424
  6.3 0.0 copy-start.1
  6.3 1.0 %copy-done.1 = bf16[512,512]{1,0:T(8,128)(2,1)S(1)} copy-done((bf16[512,512]{1,0:T(8,128)(2,1)S(1)}, bf16[512,512]{1,0:T(8,128)(2,1)}, u32[]{:S(2)}) %copy-start.1) | copy-done | bytes 524312
  7.3 0.0 copy-start.2
  7.3 1.0 %copy-done.2 = bf16[1280,128]{1,0:T(8,128)(2,1)S(1)} copy-done((bf16[1280,128]{1,0:T(8,128)(2,1)S(1)}, bf16[1280,128]{1,0:T(8,128)(2,1)}, u32[]{:S(2)}) %copy-start.2) | copy-done | bytes 327704
  8.3 0.0 copy-start.3
  8.3 0.9 %copy-done.3 = f32[128,512]{1,0:T(8,128)S(1)} copy-done((f32[128,512]{1,0:T(8,128)S(1)}, f32[128,512]{1,0:T(8,128)}, u32[]{:S(2)}) %copy-start.3) | copy-done | bytes 262168
  9.3 0.0 copy-start.4
  9.3 0.9 %copy-done.4 = bf16[2,32,1280]{2,1,0:T(8,128)(2,1)S(1)} copy-done((bf16[2,32,1280]{2,1,0:T(8,128)(2,1)S(1)}, bf16[2,32,1280]{2,1,0:T(8,128)(2,1)}, u32[]{:S(2)}) %copy-start.4) | copy-done | bytes 163864
  10.2 0.0 copy-start.5
  10.2 0.9 %copy-done.5 = f32[64,512]{1,0:T(8,128)S(1)} copy-done((f32[64,512]{1,0:T(8,128)S(1)}, f32[64,512]{1,0:T(8,128)}, u32[]{:S(2)}) %copy-start.5) | copy-done | bytes 131096
  11.1 0.0 copy-start.6
  11.1 0.8 %copy-done.6 = bf16[64,512]{1,0:T(8,128)(2,1)S(1)} copy-done((bf16[64,512]{1,0:T(8,128)(2,1)S(1)}, bf16[64,512]{1,0:T(8,128)(2,1)}, u32[]{:S(2)}) %copy-start.6) | copy-done | bytes 65560
  11.9 0.0 copy-start.7
  11.9 0.8 %copy-done.7 = bf16[128,128]{1,0:T(8,128)(2,1)S(1)} copy-done((bf16[128,128]{1,0:T(8,128)(2,1)S(1)}, bf16[128,128]{1,0:T(8,128)(2,1)}, u32[]{:S(2)}) %copy-start.7) | copy-done | bytes 32792
  12.7 0.0 copy-start.8
  12.7 0.8 %copy-done.8 = f32[16,512]{1,0:T(8,128)S(1)} copy-done((f32[16,512]{1,0:T(8,128)S(1)}, f32[16,512]{1,0:T(8,128)}, u32[]{:S(2)}) %copy-start.8) | copy-done | bytes 32792
  13.4 0.0 copy-start.9
  13.4 0.7 copy-done.9
  14.1 0.0 copy-start.10
  14.1 0.7 copy-done.10
  14.8 0.0 copy-start.11
  14.8 0.7 copy-done.11
  15.5 0.0 copy-start.12
  15.5 0.7 copy-done.12
  16.2 0.0 copy-start.13
  16.2 0.7 copy-done.13
  16.9 56.9 %shard_map.181 = bf16[2,32,512]{2,1,0:T(8,128)(2,1)S(1)} custom-call(bf16[64,1280]{1,0:T(8,128)(2,1)S(1)} %bitcast.2, f32[1280]{0:T(1024)S(1)} %copy-done.9, f32[1280]{0:T(1024)S(1)} %copy-done.10, bf16[1280,640]{1,0:T(8,128)(2,1)S(1)} %copy-done, bf16[640,1280]{1,0:T(8,128)(2,1)} %w_out_hbm.1, f32[1280]{0:T(1024)S(1)} %copy-done.11, ...), custom_call_target="tpu_custom_call" | custom-call | tf_op jit(solution)/shard_map/pallas_call | solution.py:508
  73.8 0.6 copy.25
Async XLA Ops:
  4.9 1.4 %copy-start = (bf16[1280,640]{1,0:T(8,128)(2,1)S(1)}, bf16[1280,640]{1,0:T(8,128)(2,1)}, u32[]{:S(2)}) copy-start(bf16[1280,640]{1,0:T(8,128)(2,1)} %w_in_hbm.1) | copy-start | bytes 4915204
  6.3 1.0 %copy-start.1 = (bf16[512,512]{1,0:T(8,128)(2,1)S(1)}, bf16[512,512]{1,0:T(8,128)(2,1)}, u32[]{:S(2)}) copy-start(bf16[512,512]{1,0:T(8,128)(2,1)} %constant.10.clone.waves_hbm) | copy-start | bytes 1572868
  7.3 1.0 %copy-start.2 = (bf16[1280,128]{1,0:T(8,128)(2,1)S(1)}, bf16[1280,128]{1,0:T(8,128)(2,1)}, u32[]{:S(2)}) copy-start(bf16[1280,128]{1,0:T(8,128)(2,1)} %w_embed_hbm.1) | copy-start | bytes 983044
  8.3 0.9 %copy-start.3 = (f32[128,512]{1,0:T(8,128)S(1)}, f32[128,512]{1,0:T(8,128)}, u32[]{:S(2)}) copy-start(f32[128,512]{1,0:T(8,128)} %constant.11.clone.near_ref) | copy-start | bytes 786436
  9.3 0.9 %copy-start.4 = (bf16[2,32,1280]{2,1,0:T(8,128)(2,1)S(1)}, bf16[2,32,1280]{2,1,0:T(8,128)(2,1)}, u32[]{:S(2)}) copy-start(bf16[2,32,1280]{2,1,0:T(8,128)(2,1)} %param.19) | copy-start | bytes 491524
  10.2 0.9 %copy-start.5 = (f32[64,512]{1,0:T(8,128)S(1)}, f32[64,512]{1,0:T(8,128)}, u32[]{:S(2)}) copy-start(f32[64,512]{1,0:T(8,128)} %constant.12.clone.far_ref) | copy-start | bytes 393220
  11.1 0.8 %copy-start.6 = (bf16[64,512]{1,0:T(8,128)(2,1)S(1)}, bf16[64,512]{1,0:T(8,128)(2,1)}, u32[]{:S(2)}) copy-start(bf16[64,512]{1,0:T(8,128)(2,1)} %w_proj_ref.1) | copy-start | bytes 196612
  11.9 0.8 %copy-start.7 = (bf16[128,128]{1,0:T(8,128)(2,1)S(1)}, bf16[128,128]{1,0:T(8,128)(2,1)}, u32[]{:S(2)}) copy-start(bf16[128,128]{1,0:T(8,128)(2,1)} %constant.14.clone.perm_ref) | copy-start | bytes 98308
  12.7 0.8 %copy-start.8 = (f32[16,512]{1,0:T(8,128)S(1)}, f32[16,512]{1,0:T(8,128)}, u32[]{:S(2)}) copy-start(f32[16,512]{1,0:T(8,128)} %constant.13.clone.rot_ref) | copy-start | bytes 98308
  13.4 0.7 copy-start.9
  14.1 0.7 copy-start.10
  14.8 0.7 copy-start.11
  15.5 0.7 copy-start.12
  16.2 0.7 copy-start.13

commit v2 on v1

v2 whole, which is shorter than its diff:
```python
import functools
import math

import jax
import jax.numpy as jnp
import numpy as np
from jax import lax
from jax.experimental import pallas as pl
from jax.experimental.pallas import tpu as pltpu
from jax.sharding import PartitionSpec as P

HD = 32
TILE = 128
BIG = -1e30
MESH = pl.DeviceIdType.MESH
F32 = jnp.float32
BF16 = jnp.bfloat16


def contract_last(left, right):
    return lax.dot_general(left, right, (((1,), (1,)), ((), ())), preferred_element_type=F32)


def matmul(left, right):
    return jnp.dot(left, right, preferred_element_type=F32)


def normalize(values):
    average = jnp.mean(values, axis=-1, keepdims=True)
    centered = values - average
    spread = jnp.mean(centered * centered, axis=-1, keepdims=True)
    return centered * lax.rsqrt(spread + 1e-06)


def iota(shape, dim):
    return lax.broadcasted_iota(jnp.int32, shape, dim)


def waves(count, scale, width):
    half = width // 2
    freqs = 1.0 / 10000.0 ** (np.arange(half, dtype=np.float64) / half)
    angle = (np.arange(count, dtype=np.float64) * scale)[:, None] * freqs[None, :]
    return np.concatenate([np.sin(angle), np.cos(angle)], axis=-1).astype(np.float32)


def turned(first, second):
    half = first.shape[-1] // 2
    sin_a, cos_a = first[:, :half], first[:, half:]
    sin_b, cos_b = second[:, :half], second[:, half:]
    return jnp.concatenate([sin_a * cos_b + cos_a * sin_b, cos_a * cos_b - sin_a * sin_b], axis=-1)


def picked(one_hot, table):
    high = table.astype(BF16)
    low = (table - high.astype(F32)).astype(BF16)
    return matmul(one_hot, high) + matmul(one_hot, low)


def kernel(
    cfg,
    *refs,
):
    inputs, out_ref, held = refs[:19], refs[19], refs[20:39]
    (
        part_own,
        part_send,
        rs_recv,
        enc_all,
        e_all,
        a_src,
        a_y,
        a_mid,
        a_z,
        q_src,
        q_y,
        q_mid,
        q_z,
        kv,
        kt,
        kb,
        vt,
        res_recv,
        tile_pos,
        stat_w,
        f_y,
        f_z,
        taken_ref,
        wp_all,
        att_send,
        att_recv,
        local_sem,
        x_send,
        x_recv,
        y_send,
        y_recv,
        z_send,
        z_recv,
    ) = refs[39:]
    (
        tok_ref,
        gain_ref,
        bias_ref,
        w_in,
        w_out,
        w_proj_ref,
        dest_ref,
        far_ref,
        near_ref,
        mask_ref,
        dec_gain_ref,
        wk_ref,
        wv_ref,
        wave_t,
        rot_ref,
        final_ref,
        w_embed,
        perm_ref,
        wq_ref,
    ) = held
    nx, ny, nz, images, vis = cfg
    tiles = ny * nz
    cap = TILE // tiles
    rows = images * vis
    block_rows = rows // nx
    width = out_ref.shape[2]
    cols = wq_ref.shape[0]
    own_rows = TILE // nx
    seq = lax.axis_index("seq")
    mx = lax.axis_index("mp")
    z, y = seq // ny, seq % ny

    loads = []
    for number, (src, dst) in enumerate(zip(inputs, held)):
        load = pltpu.make_async_copy(src, dst, local_sem.at[number])
        load.start()
        loads.append(load)

    def loaded(first, last):
        for load in loads[first:last]:
            load.wait()

    def partner(axis, d):
        if axis == "x":
            index = lax.rem(mx + d, nx)
            return index, {"mp": index}
        if axis == "y":
            index = lax.rem(y + d, ny)
            return index, {"seq": z * ny + index}
        index = lax.rem(z + d, nz)
        return index, {"seq": index * ny + y}

    sizes = {"x": nx, "y": ny, "z": nz}
    places = {"x": mx, "y": y, "z": z}
    sems = {"x": (x_send, x_recv), "y": (y_send, y_recv), "z": (z_send, z_recv)}
    barrier = pltpu.get_barrier_semaphore()
    for axis in "xyz":
        for d in range(1, sizes[axis]):
            pl.semaphore_signal(barrier, inc=1, device_id=partner(axis, d)[1], device_id_type=MESH)

    pending = []

    def near_first(size):
        return sorted(range(size), key=lambda d: (min(d, size - d), d))

    def exchange(axis, group, source, target):
        size = sizes[axis]
        send, recv = sems[axis]
        for d in near_first(size)[:0:-1]:
            index, device = partner(axis, d)
            copy = pltpu.make_async_remote_copy(
                src_ref=source(index),
                dst_ref=target(places[axis], d),
                send_sem=send.at[group, d - 1],
                recv_sem=recv.at[group, d - 1],
                device_id=device,
                device_id_type=MESH,
            )
            copy.start()
            pending.append(copy)

        def arrived(steps=None):
            for d in near_first(size)[1:] if steps is None else steps:
                sender, device = partner(axis, size - d)
                pltpu.make_async_remote_copy(
                    src_ref=target(sender, d),
                    dst_ref=target(sender, d),
                    send_sem=send.at[group, d - 1],
                    recv_sem=recv.at[group, d - 1],
                    device_id=device,
                    device_id_type=MESH,
                ).wait_recv()

        return arrived

    def part_of(ref, count):
        return lambda index, d=0: ref.at[pl.ds(pl.multiple_of(index * count, count), count)]

    loaded(0, 3)
    tokens = tok_ref[...].astype(F32)
    normed = (normalize(tokens) * gain_ref[...][None, :] + bias_ref[...][None, :]).astype(BF16)
    loaded(3, 4)
    pre = matmul(normed, w_in[...])
    hidden = (0.5 * pre * (1.0 + lax.erf(pre * math.sqrt(0.5)))).astype(BF16)
    loaded(4, 5)
    partial = matmul(hidden, w_out[...])
    part_own[...] = partial
    part_send[...] = partial.astype(BF16)
    pl.semaphore_wait(barrier, (nx - 1) + (ny - 1) + (nz - 1))
    rs_done = exchange("x", 0, part_of(part_send, block_rows), lambda index, d: rs_recv.at[d - 1])
    loaded(5, 6)
    wp_all[mx] = w_proj_ref[...]
    wp_done = exchange("x", 4, lambda index: wp_all.at[mx], lambda index, d: wp_all.at[index])

    loaded(6, 15)
    dest_row = jnp.concatenate([dest_ref[i] for i in range(images)], axis=1)
    eye = iota((rows, rows), 0) == iota((rows, rows), 1)
    dest_col = jnp.sum(jnp.where(eye, dest_row, 0), axis=1, keepdims=True)
    same = (dest_col == dest_row) & (iota((rows, rows), 0) // vis == iota((rows, rows), 1) // vis)
    rank_col = jnp.sum(
        jnp.where(same & (iota((rows, rows), 1) < iota((rows, rows), 0)), 1, 0), axis=1, keepdims=True
    )
    rank_row = jnp.sum(
        jnp.where(same & (iota((rows, rows), 0) < iota((rows, rows), 1)), 1, 0), axis=0, keepdims=True
    )
    slot_col = dest_col * cap + rank_col
    hits = jnp.where(slot_col == iota((rows, TILE), 1), 1.0, 0.0)
    flag_rows = jnp.zeros((16, TILE), F32)
    for i in range(images):
        count = jnp.sum(hits[i * vis : (i + 1) * vis], axis=0, keepdims=True)
        flag_rows = jnp.where(iota((16, TILE), 0) == i, count, flag_rows)

    f_y[y] = (flag_rows * BIG).astype(BF16)
    flags_y = exchange("y", 0, lambda index: f_y.at[y], lambda index, d: f_y.at[index])
    order_row = ((dest_row % ny) * nz + dest_row // ny) * cap + rank_row
    spread_f = jnp.where(order_row == iota((TILE, rows), 0), 1.0, 0.0)
    lane_image = iota((TILE, rows), 1) // vis
    spreads = [jnp.where(lane_image == i, spread_f, 0.0) for i in range(images)]
    spreads = [one.astype(BF16) for one in spreads]

    at_tile = jnp.where(dest_col == iota((rows, tiles), 1), 1.0, 0.0).astype(BF16)
    at_place = jnp.where(seq * cap + rank_col == iota((rows, TILE), 1), 1.0, 0.0).astype(BF16)
    vis_pos = turned(picked(at_tile, far_ref[...]), picked(at_place, near_ref[...]))
    tile_pos[...] = turned(near_ref[...], far_ref[pl.ds(seq, 1), :])

    mask = mask_ref[...].astype(F32)[None, :]
    dec_gain = dec_gain_ref[...][None, :]
    mask_mid = mask - jnp.mean(mask, axis=-1, keepdims=True)
    mask_spread = jnp.mean(mask_mid * mask_mid, axis=-1, keepdims=True) + 0.5
    kv_cols = 2 * cols
    gained = jnp.concatenate([wk_ref[...], wv_ref[...]], axis=0).astype(F32) * dec_gain
    stat_w[0:kv_cols, :] = gained
    gain_sum = jnp.sum(gained, axis=1, keepdims=True)
    mask_sum = jnp.sum(gained * mask_mid, axis=1, keepdims=True)
    stat_rows = iota((16, width), 0)
    stat_w[kv_cols:, :] = jnp.where(stat_rows == 0, 1.0, jnp.where(stat_rows == 1, mask_mid, 0.0)) * (1.0 / width)
    lanes = wave_t.shape[1]
    half = width // 2

    def table_step(step, carry):
        turn = rot_ref[pl.ds(step, 1), :]
        sin_t, cos_t = turn[:, :half], turn[:, half:]
        sin_w, cos_w = stat_w[:, :half], stat_w[:, half:]
        rotated = jnp.concatenate(
            [(sin_w * cos_t - cos_w * sin_t).astype(BF16), (sin_w * sin_t + cos_w * cos_t).astype(BF16)], axis=1
        )
        found = matmul(rotated, wave_t[...])
        average = found[kv_cols : kv_cols + 1]
        spread = mask_spread + 2.0 * found[kv_cols + 1 : kv_cols + 2] - average * average
        scale = lax.rsqrt(jnp.maximum(spread, 0.0) + 1e-06)
        made = ((found[:kv_cols] + mask_sum - average * gain_sum) * scale).astype(BF16)
        where = pl.ds(pl.multiple_of(step * lanes, lanes), lanes)
        kt[:, where] = made[:cols]
        vt[:, where] = made[cols:]
        return carry

    steps = rot_ref.shape[0]
    cut = [0, steps * 3 // 8, steps * 6 // 8, steps]
    lax.fori_loop(cut[0], cut[1], table_step, 0)

    loaded(15, 19)
    rs_done()
    mine = pl.ds(pl.multiple_of(mx * block_rows, block_rows), block_rows)
    mixed = tok_ref[mine, :].astype(F32) + part_own[mine, :]
    for d in range(nx - 1):
        mixed = mixed + rs_recv[d].astype(F32)
    enc_all[mine, :] = (normalize(mixed) * final_ref[...][None, :]).astype(BF16)
    enc_done = exchange(
        "x", 1, lambda index: part_of(enc_all, block_rows)(mx), lambda index, d: part_of(enc_all, block_rows)(index)
    )
    lax.fori_loop(cut[1], cut[2], table_step, 0)
    flags_y()
    joined = [f_y[i].astype(F32)[:images] for i in range(ny)]
    if ny * images < 16:
        joined.append(jnp.zeros((16 - ny * images, TILE), F32))
    f_z[z] = jnp.concatenate(joined, axis=0).astype(BF16)
    flags_z = exchange("z", 0, lambda index: f_z.at[z], lambda index, d: f_z.at[index])
    enc_done()
    embedded = matmul(enc_all[...], w_embed[...]).astype(BF16)
    e_all[mx] = embedded
    e_done = exchange("x", 2, lambda index: e_all.at[mx], lambda index, d: e_all.at[index])
    ry, rz = nz * cap, ny * cap
    a_src[...] = jnp.concatenate([matmul(one, embedded) for one in spreads], axis=1).astype(BF16)

    def first_leg(group, src, mid):
        done = exchange("y", group, part_of(src, ry), part_of(mid, ry))
        mid[pl.ds(pl.multiple_of(y * ry, ry), ry), :] = src[pl.ds(pl.multiple_of(y * ry, ry), ry), :]
        return done

    def second_leg(group, mid, turned_ref, final):
        turned_ref[...] = matmul(perm_ref[...], mid[...]).astype(BF16)
        done = exchange("z", group, part_of(turned_ref, rz), part_of(final, rz))
        final[pl.ds(pl.multiple_of(z * rz, rz), rz), :] = turned_ref[pl.ds(pl.multiple_of(z * rz, rz), rz), :]
        return done

    a_first = first_leg(1, a_src, a_y)
    lax.fori_loop(cut[2], cut[3], table_step, 0)

    score_scale = math.log2(math.e) / math.sqrt(HD)
    mask_rows = (normalize(mask + tile_pos[...]) * dec_gain).astype(BF16)
    mask_query = contract_last(mask_rows, wq_ref[...]) * score_scale

    e_done()
    full = jnp.concatenate([e_all[i] for i in range(nx)], axis=1).astype(F32)
    vis_rows = (normalize(full + vis_pos) * dec_gain).astype(BF16)
    vis_kv = contract_last(vis_rows, jnp.concatenate([wv_ref[...], wk_ref[...]], axis=0)).astype(BF16)
    for i in range(images):
        kv[i, :vis, :] = vis_kv[i * vis : (i + 1) * vis]
    axes = [("y", "z"), ("z", "y")]
    firsts, seconds = [], [[] for _ in range(images)]

    def slots(i, first, last, outer=0):
        lead = outer * sizes[axes[i][0]]
        return kv.at[i, (lead + first) * vis : (lead + last) * vis]

    def place_of(axis, d):
        return near_first(sizes[axis]).index(d)

    for i in range(images):
        one, two = axes[i]
        firsts.append(
            exchange(
                one,
                3,
                lambda index, i=i: slots(i, 0, 1),
                lambda index, d, i=i, one=one: slots(i, place_of(one, d), place_of(one, d) + 1),
            )
        )

    def forward(i, group, first, last):
        two = axes[i][1]
        seconds[i].append(
            exchange(
                two,
                group,
                lambda index: slots(i, first, last),
                lambda index, d: slots(i, first, last, place_of(two, d)),
            )
        )

    def cuts(size):
        return [(1, 3), (3, 5), (5, 8)] if size == 8 else [(1, size)]

    query = (contract_last(vis_rows, wq_ref[...]) * score_scale).astype(BF16)
    q_src[...] = jnp.concatenate([matmul(one, query) for one in spreads], axis=1).astype(BF16)
    q_first = first_leg(2, q_src, q_y)
    a_first()
    a_second = second_leg(1, a_y, a_mid, a_z)
    for i in range(images):
        forward(i, 4, 0, 1)
    for number in range(len(cuts(ny))):
        for i in range(images)[::-1]:
            if number == 0 and i == 0:
                q_first()
                q_second = second_leg(2, q_y, q_mid, q_z)
            size = sizes[axes[i][0]]
            first, last = cuts(size)[number]
            firsts[i](near_first(size)[first:last])
            forward(i, 5 + number, first, last)
    a_second()
    res_done = exchange("x", 3, part_of(a_z, own_rows), lambda index, d: res_recv.at[index])
    res_recv[mx] = a_z[pl.ds(pl.multiple_of(mx * own_rows, own_rows), own_rows), :]

    flags_z()
    bias_row, bias_from = iota((ny * 16, 16), 0), iota((ny * 16, 16), 1)
    unpack = jnp.where(
        (bias_row % 16 < images) & (bias_from == (bias_row // 16) * images + bias_row % 16), 1.0, 0.0
    ).astype(BF16)
    for zs in range(nz):
        part = matmul(unpack, f_z[zs]).astype(BF16)
        for ys in range(ny):
            kb[:, (zs * ny + ys) * TILE : (zs * ny + ys + 1) * TILE] = part[ys * 16 : (ys + 1) * 16]
    every_flag = jnp.concatenate([f_z[zs] for zs in range(nz)], axis=0)
    slot_row, slot_from = iota((TILE, nz * 16), 0), iota((TILE, nz * 16), 1)
    source_row = slot_row // cap
    here_lane = iota((TILE, TILE), 1) == seq * cap + iota((TILE, TILE), 0) % cap
    presents = []
    for i in range(images):
        choose = jnp.where(slot_from == (source_row // ny) * 16 + (source_row % ny) * images + i, 1.0, 0.0)
        seen = jnp.where(here_lane, matmul(choose.astype(BF16), every_flag), 0.0)
        presents.append(jnp.where(jnp.sum(seen, axis=1, keepdims=True) < -1.0, 1.0, 0.0))
    taken_ref[...] = jnp.concatenate([jnp.broadcast_to(one, (TILE, TILE)) for one in presents], axis=1)
    q_second()
    lane = iota((TILE, cols), 1)
    head_masks = [jnp.where(lane // HD == h, 1.0, 0.0) for h in range(cols // HD)]
    heads = len(head_masks)
    found_q = q_z[...]
    block = math.gcd(2048, tiles * TILE)
    lookups = []
    stacked = []
    for i in range(images):
        here = jnp.where(presents[i] > 0, found_q[:, i * cols : (i + 1) * cols].astype(F32), mask_query)
        stacked.append(jnp.concatenate([here * one for one in head_masks], axis=0).astype(BF16))

    def fold(state, scores, values_of):
        top, total, accum = state
        new_top = jnp.maximum(top, jnp.max(scores, axis=1, keepdims=True))
        fix = jnp.exp2(top - new_top)
        expo = jnp.exp2(scores - new_top)
        total = total * fix + jnp.sum(expo, axis=1, keepdims=True)
        accum = accum * fix + values_of(expo.astype(BF16))
        return new_top, total, accum

    for i in range(images):
        select = jnp.where(iota((heads * TILE, 16), 1) == i, 1.0, 0.0).astype(BF16)
        lookups.append(jnp.concatenate([stacked[i], select], axis=1))

    def masked_block(number, states):
        where = pl.ds(pl.multiple_of(number * block, block), block)
        keys = jnp.concatenate([kt[:, where], kb[:, where]], axis=0)
        scores = [matmul(one, keys) for one in lookups]
        return tuple(
            fold(state, one, lambda expo: contract_last(expo, vt[:, where])) for state, one in zip(states, scores)
        )

    start = (
        jnp.full((heads * TILE, 1), BIG, F32),
        jnp.zeros((heads * TILE, 1), F32),
        jnp.zeros((heads * TILE, cols), F32),
    )
    states = lax.fori_loop(0, tiles * TILE // block, masked_block, (start,) * images)

    lookups = [jnp.concatenate([jnp.zeros_like(one), one], axis=1) for one in stacked]

    def visible(states, first, last):
        spans = [slice(first * sizes[axes[i][0]] * vis, last * sizes[axes[i][0]] * vis) for i in range(images)]
        scores = [contract_last(lookups[i], kv[i, spans[i], :]) for i in range(images)]
        return [
            fold(states[i], scores[i], lambda expo, i=i: matmul(expo, kv[i, spans[i], :])[:, :cols])
            for i in range(images)
        ]

    near = 5 if nz == 8 else 1
    for first, last in ((0, near), (near, nz)):
        for i in range(images):
            for second in seconds[i]:
                second(near_first(sizes[axes[i][1]])[max(first, 1) : last])
        states = visible(states, first, last)
    gathered = []
    for i in range(images):
        top, total, accum = states[i]
        accum = accum / total
        attended = jnp.zeros((TILE, cols), F32)
        for h in range(heads):
            attended = attended + accum[h * TILE : (h + 1) * TILE] * head_masks[h]
        gathered.append(attended)
    att_send[...] = jnp.concatenate(gathered, axis=1).astype(BF16)
    att_done = exchange("x", 5, part_of(att_send, own_rows), lambda index, d: att_recv.at[index])
    tile_mine = pl.ds(pl.multiple_of(mx * own_rows, own_rows), own_rows)
    att_recv[mx] = att_send[tile_mine, :]

    res_done()
    my_pos = tile_pos[tile_mine, :]
    chunk = width // nx
    bases = []
    for i in range(images):
        rows_here = jnp.concatenate(
            [res_recv[j, :, i * chunk : (i + 1) * chunk] for j in range(nx)], axis=1
        ).astype(F32)
        present = taken_ref[tile_mine, i * TILE : i * TILE + 1]
        bases.append(jnp.where(present > 0, rows_here, mask) + my_pos)
    wp_done()
    att_done()
    sums = jnp.concatenate(bases, axis=0)
    for j in range(nx):
        pieces = [att_recv[j, :, i * cols : (i + 1) * cols] for i in range(images)]
        sums = sums + matmul(jnp.concatenate(pieces, axis=0), wp_all[j])
    for i in range(images):
        out_ref[i] = sums[i * own_rows : (i + 1) * own_rows].astype(BF16)
    for copy in pending:
        copy.wait_send()


def local(
    enc_tokens,
    enc_gain,
    enc_bias,
    w_in,
    w_out,
    final_gain,
    w_embed,
    dest,
    mask_token,
    dec_gain,
    w_query,
    w_key,
    w_value,
    w_proj,
):
    images, vis, model_width = enc_tokens.shape
    seq_count = lax.axis_size("seq")
    nx = lax.axis_size("mp")
    ny = math.isqrt(seq_count)
    nz = seq_count // ny
    width = mask_token.shape[0]
    cols = w_query.shape[1]
    cap = TILE // seq_count
    rows = images * vis
    own = TILE // nx
    patches = seq_count * TILE

    low = min(4, seq_count // 2)
    s_low, t, c = np.meshgrid(np.arange(low), np.arange(seq_count), np.arange(cap), indexing="ij")
    place = (s_low * cap + t * TILE + c).reshape(-1)
    wave_t = waves(int(place.max()) + 1, 1, width)[place].T.astype(jnp.bfloat16)
    near = waves(TILE, 1, width)
    far = waves(seq_count, TILE, width)
    rot = waves(seq_count // low, low * cap, width)
    zi, yi, ci = np.meshgrid(np.arange(nz), np.arange(ny), np.arange(cap), indexing="ij")
    perm = np.zeros((TILE, TILE), np.float32)
    perm[np.arange(TILE), ((yi * nz + zi) * cap + ci).reshape(-1)] = 1.0

    hbm = pl.BlockSpec(memory_space=pltpu.HBM)
    vmem = pl.BlockSpec(memory_space=pltpu.VMEM)
    operands = (
        enc_tokens.reshape(rows, model_width),
        enc_gain,
        enc_bias,
        w_in,
        w_out,
        w_proj,
        dest.transpose(0, 2, 1),
        jnp.asarray(far),
        jnp.asarray(near),
        mask_token,
        dec_gain,
        w_key.T,
        w_value.T,
        jnp.asarray(wave_t),
        jnp.asarray(rot),
        final_gain,
        w_embed,
        jnp.asarray(perm, BF16),
        w_query.T,
    )
    block_rows = rows // nx
    dma = pltpu.SemaphoreType.DMA
    scratch = [
        *[pltpu.VMEM(operand.shape, operand.dtype) for operand in operands],
        pltpu.VMEM((rows, model_width), F32),
        pltpu.VMEM((rows, model_width), BF16),
        pltpu.VMEM((nx - 1, block_rows, model_width), BF16),
        pltpu.VMEM((rows, model_width), BF16),
        pltpu.VMEM((nx, rows, width // nx), BF16),
        *[pltpu.VMEM((TILE, images * width // nx), BF16)] * 4,
        *[pltpu.VMEM((TILE, images * cols), BF16)] * 4,
        pltpu.VMEM((images, seq_count * vis, 2 * cols), BF16),
        pltpu.VMEM((cols, patches), BF16),
        pltpu.VMEM((16, patches), BF16),
        pltpu.VMEM((cols, patches), BF16),
        pltpu.VMEM((nx, own, images * width // nx), BF16),
        pltpu.VMEM((TILE, width), F32),
        pltpu.VMEM((2 * cols + 16, width), F32),
        pltpu.VMEM((ny, 16, TILE), BF16),
        pltpu.VMEM((nz, 16, TILE), BF16),
        pltpu.VMEM((TILE, images * TILE), F32),
        pltpu.VMEM((nx, cols, width), BF16),
        pltpu.VMEM((TILE, images * cols), BF16),
        pltpu.VMEM((nx, own, images * cols), BF16),
        dma((len(operands),)),
        dma((6, nx - 1)),
        dma((6, nx - 1)),
        dma((8, ny - 1)),
        dma((8, ny - 1)),
        dma((8, nz - 1)),
        dma((8, nz - 1)),
    ]
    return pl.pallas_call(
        functools.partial(kernel, (nx, ny, nz, images, vis)),
        out_shape=pltpu.VMEM((images, own, width), BF16),
        in_specs=[hbm] * len(operands),
        out_specs=vmem,
        scratch_shapes=scratch,
        compiler_params=pltpu.CompilerParams(
            collective_id=0, has_side_effects=True, vmem_limit_bytes=63300000
        ),
    )(*operands)


def solution(mesh):
    placed = (
        P("dp", "seq", None),
        P(),
        P(),
        P(None, "mp"),
        P("mp", None),
        P(),
        P(None, "mp"),
        P("dp", "seq", None),
        P(),
        P(),
        P(None, "mp"),
        P(None, "mp"),
        P(None, "mp"),
        P("mp", None),
    )
    return jax.shard_map(
        local, mesh=mesh, in_specs=placed, out_specs=P("dp", ("seq", "mp"), None), check_vma=False
    )
```

time: 75.2 us -> 54.3 us (0.72)
  local copies, waits for them, and re-layouts: 16.1 us -> 0.63 us
  Pallas kernels: 56.9 us -> 53.5 us
  other arithmetic: 1.34 us -> 0 us
    unnamed x33 -> x1, local copies, waits for them, and re-layouts: 16 us -> 0.63 us
    pallas_call x1, Pallas kernels: 56.9 us -> 53.5 us  [local(): pl.pallas_call(functools.partial(kernel, (nx, ny, nz, images, vis)), out_...]
    unnamed x1 -> x0, other arithmetic: 1.34 us -> none
where the time goes in v2:
time: 54.3 us; the launch traced here: 54.2 us
  Pallas kernels  53.5 us (99%)
  local copies, waits for them, and re-layouts  0.63 us (1%)
    pallas_call x1, Pallas kernels, local(): pl.pallas_call(functools.partial(kernel, (nx, ny, nz, images, vis)), out_...  53.5 us

profile of v2, /device:TPU:8, one launch (start us, length us, event | category | flops | bytes accessed | tf_op | source)
XLA Modules:
  0.0 54.2 jit_solution(8170229971971995538)
XLA Ops:
  0.0 53.5 %shard_map.181 = bf16[2,32,512]{2,1,0:T(8,128)(2,1)S(1)} custom-call(bf16[64,1280]{1,0:T(8,128)(2,1)} %bitcast.7, f32[1280]{0:T(1024)} %refs_1_.1, f32[1280]{0:T(1024)} %refs_2_.1, bf16[1280,640]{1,0:T(8,128)(2,1)} %refs_3_.1, bf16[640,1280]{1,0:T(8,128)(2,1)} %refs_4_.1, bf16[64,512]{1,0:T(8,128)(2,1)} %refs_5_.1, s32[2,1,32]{2,1,0:T(1,128)} %bitcast.11, ...), custom_call_target="tpu_custom_call" | custom-call | tf_op jit(solution)/shard_map/pallas_call | solution.py:587
  53.5 0.6 %copy.22 = bf16[2,32,512]{2,1,0:T(8,128)(2,1)} copy(bf16[2,32,512]{2,1,0:T(8,128)(2,1)S(1)} %shard_map.181) | data formatting | bytes 131072

commit v3 on v2

--- a/solution.py
+++ b/solution.py
@@ -131,9 +131,13 @@
 
     loads = []
     for number, (src, dst) in enumerate(zip(inputs, held)):
-        load = pltpu.make_async_copy(src, dst, local_sem.at[number])
-        load.start()
-        loads.append(load)
+        loads.append(pltpu.make_async_copy(src, dst, local_sem.at[number]))
+
+    def load_now(first, last):
+        for load in loads[first:last]:
+            load.start()
+
+    load_now(0, 5)
 
     def loaded(first, last):
         for load in loads[first:last]:
@@ -195,6 +199,7 @@
     def part_of(ref, count):
         return lambda index, d=0: ref.at[pl.ds(pl.multiple_of(index * count, count), count)]
 
+    load_now(5, len(loads))
     loaded(0, 3)
     tokens = tok_ref[...].astype(F32)
     normed = (normalize(tokens) * gain_ref[...][None, :] + bias_ref[...][None, :]).astype(BF16)
@@ -425,7 +430,7 @@
         lookups.append(jnp.concatenate([stacked[i], select], axis=1))
 
     def masked_block(number, states):
-        where = pl.ds(pl.multiple_of(number * block, block), block)
+        where = slice(number * block, (number + 1) * block)
         keys = jnp.concatenate([kt[:, where], kb[:, where]], axis=0)
         scores = [matmul(one, keys) for one in lookups]
         return tuple(
@@ -437,7 +442,9 @@
         jnp.zeros((heads * TILE, 1), F32),
         jnp.zeros((heads * TILE, cols), F32),
     )
-    states = lax.fori_loop(0, tiles * TILE // block, masked_block, (start,) * images)
+    states = (start,) * images
+    for number in range(tiles * TILE // block):
+        states = masked_block(number, states)
 
     lookups = [jnp.concatenate([jnp.zeros_like(one), one], axis=1) for one in stacked]
 
@@ -464,6 +471,7 @@
             attended = attended + accum[h * TILE : (h + 1) * TILE] * head_masks[h]
         gathered.append(attended)
     att_send[...] = jnp.concatenate(gathered, axis=1).astype(BF16)
+    sent = len(pending)
     att_done = exchange("x", 5, part_of(att_send, own_rows), lambda index, d: att_recv.at[index])
     tile_mine = pl.ds(pl.multiple_of(mx * own_rows, own_rows), own_rows)
     att_recv[mx] = att_send[tile_mine, :]
@@ -478,6 +486,8 @@
         ).astype(F32)
         present = taken_ref[tile_mine, i * TILE : i * TILE + 1]
         bases.append(jnp.where(present > 0, rows_here, mask) + my_pos)
+    for copy in pending[:sent]:
+        copy.wait_send()
     wp_done()
     att_done()
     sums = jnp.concatenate(bases, axis=0)
@@ -486,7 +496,7 @@
         sums = sums + matmul(jnp.concatenate(pieces, axis=0), wp_all[j])
     for i in range(images):
         out_ref[i] = sums[i * own_rows : (i + 1) * own_rows].astype(BF16)
-    for copy in pending:
+    for copy in pending[sent:]:
         copy.wait_send()
 
 

time: 54.3 us -> 52.5 us (0.967)
  Pallas kernels: 53.5 us -> 51.7 us
    pallas_call x1, Pallas kernels: 53.5 us -> 51.7 us  [local(): pl.pallas_call(functools.partial(kernel, (nx, ny, nz, images, vis)), out_...]
where the time goes in v3:
time: 52.5 us; the launch traced here: 52.4 us
  Pallas kernels  51.7 us (98%)
  local copies, waits for them, and re-layouts  0.63 us (1%)
    pallas_call x1, Pallas kernels, local(): pl.pallas_call(functools.partial(kernel, (nx, ny, nz, images, vis)), out_...  51.7 us

profile of v3, /device:TPU:8, one launch (start us, length us, event | category | flops | bytes accessed | tf_op | source)
XLA Modules:
  0.0 52.4 jit_solution(4871697621233415360)
XLA Ops:
  0.0 51.7 %shard_map.181 = bf16[2,32,512]{2,1,0:T(8,128)(2,1)S(1)} custom-call(bf16[64,1280]{1,0:T(8,128)(2,1)} %bitcast.7, f32[1280]{0:T(1024)} %refs_1_.1, f32[1280]{0:T(1024)} %refs_2_.1, bf16[1280,640]{1,0:T(8,128)(2,1)} %refs_3_.1, bf16[640,1280]{1,0:T(8,128)(2,1)} %refs_4_.1, bf16[64,512]{1,0:T(8,128)(2,1)} %refs_5_.1, s32[2,1,32]{2,1,0:T(1,128)} %bitcast.11, ...), custom_call_target="tpu_custom_call" | custom-call | tf_op jit(solution)/shard_map/pallas_call | solution.py:597
  51.7 0.6 %copy.22 = bf16[2,32,512]{2,1,0:T(8,128)(2,1)} copy(bf16[2,32,512]{2,1,0:T(8,128)(2,1)S(1)} %shard_map.181) | data formatting | bytes 131072

commit v4 on v3

--- a/solution.py
+++ b/solution.py
@@ -166,10 +166,12 @@
     def near_first(size):
         return sorted(range(size), key=lambda d: (min(d, size - d), d))
 
-    def exchange(axis, group, source, target):
+    def exchange(axis, group, source, target, steps=None):
         size = sizes[axis]
         send, recv = sems[axis]
-        for d in near_first(size)[:0:-1]:
+        steps = near_first(size)[1:] if steps is None else steps
+        open_steps = list(steps)
+        for d in steps[::-1]:
             index, device = partner(axis, d)
             copy = pltpu.make_async_remote_copy(
                 src_ref=source(index),
@@ -182,8 +184,9 @@
             copy.start()
             pending.append(copy)
 
-        def arrived(steps=None):
-            for d in near_first(size)[1:] if steps is None else steps:
+        def arrived(wanted=steps):
+            for d in [d for d in wanted if d in open_steps]:
+                open_steps.remove(d)
                 sender, device = partner(axis, size - d)
                 pltpu.make_async_remote_copy(
                     src_ref=target(sender, d),
@@ -327,6 +330,9 @@
     e_done()
     full = jnp.concatenate([e_all[i] for i in range(nx)], axis=1).astype(F32)
     vis_rows = (normalize(full + vis_pos) * dec_gain).astype(BF16)
+    query = (contract_last(vis_rows, wq_ref[...]) * score_scale).astype(BF16)
+    q_src[...] = jnp.concatenate([matmul(one, query) for one in spreads], axis=1).astype(BF16)
+    q_first = first_leg(2, q_src, q_y)
     vis_kv = contract_last(vis_rows, jnp.concatenate([wv_ref[...], wk_ref[...]], axis=0)).astype(BF16)
     for i in range(images):
         kv[i, :vis, :] = vis_kv[i * vis : (i + 1) * vis]
@@ -351,7 +357,7 @@
             )
         )
 
-    def forward(i, group, first, last):
+    def forward(i, group, first, last, steps=None):
         two = axes[i][1]
         seconds[i].append(
             exchange(
@@ -359,19 +365,54 @@
                 group,
                 lambda index: slots(i, first, last),
                 lambda index, d: slots(i, first, last, place_of(two, d)),
+                steps,
             )
         )
 
+    def relay(i, group, first, last, carried):
+        two = axes[i][1]
+        send, recv = sems[two]
+        copies = {}
+        for second in carried:
+            second([2, 6])
+        for total, via in ((4, 2), (3, 2), (5, 6)):
+            copies[total] = pltpu.make_async_remote_copy(
+                src_ref=slots(i, first, last, place_of(two, via)),
+                dst_ref=slots(i, first, last, place_of(two, total)),
+                send_sem=send.at[group, total - 1],
+                recv_sem=recv.at[group, total - 1],
+                device_id=partner(two, (total - via) % sizes[two])[1],
+                device_id_type=MESH,
+            )
+            copies[total].start()
+            pending.append(copies[total])
+
+        def arrived(wanted):
+            for d in [d for d in wanted if d in copies]:
+                back = partner(two, sizes[two] - d)[1]
+                pltpu.make_async_remote_copy(
+                    src_ref=slots(i, first, last, place_of(two, d)),
+                    dst_ref=slots(i, first, last, place_of(two, d)),
+                    send_sem=send.at[group, d - 1],
+                    recv_sem=recv.at[group, d - 1],
+                    device_id=back,
+                    device_id_type=MESH,
+                ).wait_recv()
+                del copies[d]
+
+        return arrived
+
+    relayed = ny == 8 and nz == 8
+    close = [1, 7, 2, 6] if relayed else None
+    relays = [[] for _ in range(images)]
+
     def cuts(size):
         return [(1, 3), (3, 5), (5, 8)] if size == 8 else [(1, size)]
 
-    query = (contract_last(vis_rows, wq_ref[...]) * score_scale).astype(BF16)
-    q_src[...] = jnp.concatenate([matmul(one, query) for one in spreads], axis=1).astype(BF16)
-    q_first = first_leg(2, q_src, q_y)
     a_first()
     a_second = second_leg(1, a_y, a_mid, a_z)
     for i in range(images):
-        forward(i, 4, 0, 1)
+        forward(i, 4, 0, 1, close)
     for number in range(len(cuts(ny))):
         for i in range(images)[::-1]:
             if number == 0 and i == 0:
@@ -380,7 +421,7 @@
             size = sizes[axes[i][0]]
             first, last = cuts(size)[number]
             firsts[i](near_first(size)[first:last])
-            forward(i, 5 + number, first, last)
+            forward(i, 5 + number, first, last, close if number < 2 else None)
     a_second()
     res_done = exchange("x", 3, part_of(a_z, own_rows), lambda index, d: res_recv.at[index])
     res_recv[mx] = a_z[pl.ds(pl.multiple_of(mx * own_rows, own_rows), own_rows), :]
@@ -403,6 +444,9 @@
         choose = jnp.where(slot_from == (source_row // ny) * 16 + (source_row % ny) * images + i, 1.0, 0.0)
         seen = jnp.where(here_lane, matmul(choose.astype(BF16), every_flag), 0.0)
         presents.append(jnp.where(jnp.sum(seen, axis=1, keepdims=True) < -1.0, 1.0, 0.0))
+    if relayed:
+        for i in range(images)[::-1]:
+            relays[i].append(relay(i, 8, 0, 3, seconds[i][:2]))
     taken_ref[...] = jnp.concatenate([jnp.broadcast_to(one, (TILE, TILE)) for one in presents], axis=1)
     q_second()
     lane = iota((TILE, cols), 1)
@@ -445,6 +489,9 @@
     states = (start,) * images
     for number in range(tiles * TILE // block):
         states = masked_block(number, states)
+        if relayed and number == 0:
+            for i in range(images)[::-1]:
+                relays[i].append(relay(i, 9, 3, 5, seconds[i][2:3]))
 
     lookups = [jnp.concatenate([jnp.zeros_like(one), one], axis=1) for one in stacked]
 
@@ -459,7 +506,7 @@
     near = 5 if nz == 8 else 1
     for first, last in ((0, near), (near, nz)):
         for i in range(images):
-            for second in seconds[i]:
+            for second in seconds[i] + relays[i]:
                 second(near_first(sizes[axes[i][1]])[max(first, 1) : last])
         states = visible(states, first, last)
     gathered = []
@@ -589,10 +636,10 @@
         dma((len(operands),)),
         dma((6, nx - 1)),
         dma((6, nx - 1)),
-        dma((8, ny - 1)),
-        dma((8, ny - 1)),
-        dma((8, nz - 1)),
-        dma((8, nz - 1)),
+        dma((10, ny - 1)),
+        dma((10, ny - 1)),
+        dma((10, nz - 1)),
+        dma((10, nz - 1)),
     ]
     return pl.pallas_call(
         functools.partial(kernel, (nx, ny, nz, images, vis)),

time: 52.5 us -> 51.7 us (0.985)
  the two profiles are of different devices: /device:TPU:8 before, /device:TPU:2 now
where the time goes in v4:
time: 51.7 us; the launch traced here: 51.6 us
  Pallas kernels  51 us (99%)
  local copies, waits for them, and re-layouts  0.63 us (1%)
    pallas_call x1, Pallas kernels, local(): pl.pallas_call(functools.partial(kernel, (nx, ny, nz, images, vis)), out_...  51 us

profile of v4, /device:TPU:2, one launch (start us, length us, event | category | flops | bytes accessed | tf_op | source)
XLA Modules:
  0.0 51.6 jit_solution(18089572916015074934)
XLA Ops:
  0.0 51.0 %shard_map.181 = bf16[2,32,512]{2,1,0:T(8,128)(2,1)S(1)} custom-call(bf16[64,1280]{1,0:T(8,128)(2,1)} %bitcast.7, f32[1280]{0:T(1024)} %refs_1_.1, f32[1280]{0:T(1024)} %refs_2_.1, bf16[1280,640]{1,0:T(8,128)(2,1)} %refs_3_.1, bf16[640,1280]{1,0:T(8,128)(2,1)} %refs_4_.1, bf16[64,512]{1,0:T(8,128)(2,1)} %refs_5_.1, s32[2,1,32]{2,1,0:T(1,128)} %bitcast.11, ...), custom_call_target="tpu_custom_call" | custom-call | tf_op jit(solution)/shard_map/pallas_call | solution.py:644
  51.0 0.6 %copy.22 = bf16[2,32,512]{2,1,0:T(8,128)(2,1)} copy(bf16[2,32,512]{2,1,0:T(8,128)(2,1)S(1)} %shard_map.181) | data formatting | bytes 131072

commit v5 on v4

--- a/solution.py
+++ b/solution.py
@@ -330,10 +330,11 @@
     e_done()
     full = jnp.concatenate([e_all[i] for i in range(nx)], axis=1).astype(F32)
     vis_rows = (normalize(full + vis_pos) * dec_gain).astype(BF16)
-    query = (contract_last(vis_rows, wq_ref[...]) * score_scale).astype(BF16)
+    joint = contract_last(vis_rows, jnp.concatenate([wv_ref[...], wk_ref[...], wq_ref[...]], axis=0))
+    query = (joint[:, kv_cols:] * score_scale).astype(BF16)
     q_src[...] = jnp.concatenate([matmul(one, query) for one in spreads], axis=1).astype(BF16)
     q_first = first_leg(2, q_src, q_y)
-    vis_kv = contract_last(vis_rows, jnp.concatenate([wv_ref[...], wk_ref[...]], axis=0)).astype(BF16)
+    vis_kv = joint[:, :kv_cols].astype(BF16)
     for i in range(images):
         kv[i, :vis, :] = vis_kv[i * vis : (i + 1) * vis]
     axes = [("y", "z"), ("z", "y")]

time: 51.7 us -> 51.9 us (level)
  the two profiles are of different devices: /device:TPU:2 before, /device:TPU:64 now
where the time goes in v5:
time: 51.9 us; the launch traced here: 51.8 us
  Pallas kernels  51.2 us (99%)
  local copies, waits for them, and re-layouts  0.63 us (1%)
    pallas_call x1, Pallas kernels, local(): pl.pallas_call(functools.partial(kernel, (nx, ny, nz, images, vis)), out_...  51.2 us

profile of v5, /device:TPU:64, one launch (start us, length us, event | category | flops | bytes accessed | tf_op | source)
XLA Modules:
  0.0 51.8 jit_solution(14722269692116800622)
XLA Ops:
  0.0 51.2 %shard_map.181 = bf16[2,32,512]{2,1,0:T(8,128)(2,1)S(1)} custom-call(bf16[64,1280]{1,0:T(8,128)(2,1)} %bitcast.7, f32[1280]{0:T(1024)} %refs_1_.1, f32[1280]{0:T(1024)} %refs_2_.1, bf16[1280,640]{1,0:T(8,128)(2,1)} %refs_3_.1, bf16[640,1280]{1,0:T(8,128)(2,1)} %refs_4_.1, bf16[64,512]{1,0:T(8,128)(2,1)} %refs_5_.1, s32[2,1,32]{2,1,0:T(1,128)} %bitcast.11, ...), custom_call_target="tpu_custom_call" | custom-call | tf_op jit(solution)/shard_map/pallas_call | solution.py:645
  51.2 0.6 %copy.22 = bf16[2,32,512]{2,1,0:T(8,128)(2,1)} copy(bf16[2,32,512]{2,1,0:T(8,128)(2,1)S(1)} %shard_map.181) | data formatting | bytes 131072
